TPU v7x, 32 devices: a whole 2x2x4 slice. The times are simulated.
32 devices in a mesh: ktot: 8 (over y, x, core), kvir: 4 (over z).
Axes of the slice: x: 2, y: 2, z: 4, core: 2. Of those that a mesh axis runs over, the one named last changes fastest.
Arguments:
- amplitudes: bfloat16 [8, 4, 672, 1024], P('ktot', 'kvir'), may hold values from -6 to 6
- ladder_integrals: bfloat16 [8, 4, 1024, 1024], P('ktot', 'kvir'), may hold values from -0.09375 to 0.09375
- listed: int32 [8, 4], P('ktot', 'kvir'), may hold values 0 or 1
- current: bfloat16 [8, 672, 1024], P('ktot', 'kvir'), may hold values from -3 to 3
- denominators: float32 [8, 672, 1024], P('ktot', 'kvir'), may hold values from 2 to 8
- cycle_integrals: bfloat16 [8, 512, 512], P('ktot', 'kvir'), may hold values from -0.25 to 0.25
Outputs:
- ladder_res: bfloat16 [8, 672, 1024], P('ktot', 'kvir')
- cycle_res: float32 [8, 1344, 1344], P('ktot', 'kvir')
All inputs are finite; a program needn't handle non-finite values. No bound on the sum of `listed` on one device may be relied on, other than what follows from the above.
Results may differ from a plain program's by a relative error of at most 0.017.
Values may be sent and summed in bfloat16 or wider, within the bound.
A program may use at most 64 MiB of HBM per device.

v0:
```python
import jax
import jax.numpy as jnp
from jax import lax
from jax.sharding import PartitionSpec as P


def shards(amplitudes, ladder_integrals, listed, current, denominators, cycle_integrals):
    amp_block = amplitudes[0, 0]
    weights = ladder_integrals[0, 0]
    scale_mask = listed[0, 0].astype(jnp.float32)
    rows_dev = current.shape[1]
    width = current.shape[2]
    tot_count = lax.axis_size("ktot")
    vir_count = lax.axis_size("kvir")
    summed = lax.psum(
        jnp.dot(amp_block, weights, preferred_element_type=jnp.float32) * scale_mask, "kvir"
    )
    ladder = lax.dynamic_slice_in_dim(summed, lax.axis_index("kvir") * rows_dev, rows_dev, 0)
    updated = (current[0].astype(jnp.float32) + ladder / denominators[0]).astype(jnp.bfloat16)
    col_width = width // tot_count
    received = lax.all_to_all(
        updated.reshape(rows_dev, tot_count, col_width),
        "ktot",
        split_axis=1,
        concat_axis=1,
        tiled=True,
    )
    local_cycle = received.reshape(rows_dev * tot_count, col_width)
    cycle_rows = local_cycle.shape[0]
    cycle_weights = cycle_integrals[0]
    cycle_width = cycle_weights.shape[1]
    share_rows = cycle_rows // vir_count
    my_start = lax.axis_index("kvir") * share_rows
    full_matrix, full_weights = (
        lax.all_gather(local_cycle, "kvir", axis=1, tiled=True),
        lax.all_gather(cycle_weights, "kvir", axis=0, tiled=True),
    )
    my_rows = lax.dynamic_slice_in_dim(full_matrix, my_start, share_rows, 0)
    row_parts = my_rows.reshape(share_rows, vir_count, col_width)
    weight_parts = full_weights.reshape(vir_count, col_width, cycle_width)
    terms = jnp.einsum("svw,vwc->vsc", row_parts, weight_parts, preferred_element_type=jnp.float32)
    terms = terms.astype(jnp.bfloat16).astype(jnp.float32)
    cycle_mixed = jnp.sum(terms, axis=0).astype(jnp.bfloat16)
    cycle_out = lax.dot_general(
        cycle_mixed, full_matrix, (((1,), (1,)), ((), ())), preferred_element_type=jnp.float32
    )
    return (ladder.astype(jnp.bfloat16)[None], (cycle_out * cycle_width ** (-0.5))[None])


def solution(mesh):
    return jax.shard_map(
        shards,
        mesh=mesh,
        in_specs=(
            P("ktot", "kvir", None, None),
            P("ktot", "kvir", None, None),
            P("ktot", "kvir"),
            P("ktot", "kvir", None),
            P("ktot", "kvir", None),
            P("ktot", "kvir", None),
        ),
        out_specs=(P("ktot", "kvir", None), P("ktot", "kvir", None)),
        check_vma=False,
    )
```

profile of v0, /device:TPU:0, one launch (start us, length us, event | category | flops | bytes accessed | tf_op | source)
XLA Modules:
  0.0 186.2 jit_solution(12479144459914517773)
XLA Ops:
  7.2 0.0 copy-start
  7.2 0.0 all-reduce.2.cloned.1.call-start
  8.0 0.8 copy-done
  8.8 4.5 %fusion.3 = f32[672,1024]{1,0:T(8,128)} fusion(bf16[1,1,1024,1024]{3,2,1,0:T(8,128)(2,1)S(1)} %copy-done, bf16[1,1,672,1024]{3,2,1,0:T(8,128)(2,1)} %param.6, f32[]{:T(128)} %bitcast.2), kind=kOutput, calls=%fused_computation.4 | convolution fusion | flops 1409974272 | bytes 6225924 | tf_op jit(solution)/shard_map/dot_general | solution.py:16
  13.3 0.0 copy-start.2
  13.3 0.0 copy-start.3
  13.3 0.0 all-reduce.2.cloned.1.call-update
  13.3 0.0 all-gather.3.cloned.1.call-start
  13.4 0.0 copy-start.4
  13.4 111.2 %all-reduce.2.cloned.1.call-done = f32[672,1024]{1,0:T(8,128)} async-done(((f32[672,1024]{1,0:T(8,128)}), f32[672,1024]{1,0:T(8,128)}) %all-reduce.2.cloned.1.call-update) | async-done | bytes 2752528 | tf_op jit(solution)/shard_map/psum | solution.py:15
  124.5 0.0 copy-done.2
  124.5 0.0 copy-done.3
  124.5 1.2 copy_bitcast_fusion
  125.8 11.3 %all_to_all.5 = bf16[168,8,128]{2,0,1:T(8,128)(2,1)S(1)} all-to-all(bf16[168,8,128]{2,0,1:T(8,128)(2,1)S(1)} %copy_bitcast_fusion), channel_id=1, replica_groups=mesh['ktot'=8,'kvir'=4] {'ktot'}, dimensions={1} | all-to-all | bytes 688128 | tf_op jit(solution)/shard_map/all_to_all | solution.py:21
  137.0 0.8 copy.22
  137.8 0.0 all-gather.3.cloned.1.call-update
  137.8 0.0 copy-done.4
  137.8 20.6 %all-gather = bf16[1,512,512]{2,1,0:T(8,128)(2,1)S(1)} all-gather(bf16[1,128,512]{2,1,0:T(8,128)(2,1)S(1)} %copy-done.4), channel_id=2, replica_groups=mesh['ktot'=8,'kvir'=4] {'kvir'}, dimensions={1}, use_global_device_ids=true | all-gather | bytes 655360 | tf_op jit(solution)/shard_map/all_gather | solution.py:36
  158.4 1.9 %fusion.9 = bf16[1,168,1024]{2,1,0:T(8,128)(2,1)} fusion(f32[672,1024]{1,0:T(8,128)} %all-reduce.2.cloned.1.call-done, s32[]{:T(128)S(6)} %select_n.6), kind=kLoop, calls=%fused_computation.12 | loop fusion | bytes 688132 | tf_op jit(solution)/shard_map/broadcast_in_dim | solution.py:47
  160.3 15.5 %all-gather.3.cloned.1.call-done = bf16[1344,512]{1,0:T(8,128)(2,1)} async-done(((bf16[1344,128]{1,0:T(8,128)(2,1)}), bf16[1344,512]{1,0:T(8,128)(2,1)}) %all-gather.3.cloned.1.call-update) | async-done | bytes 1376272 | tf_op jit(solution)/shard_map/all_gather | solution.py:35
  175.8 0.0 copy-start.1
  175.8 1.6 fusion.7
  177.4 0.0 copy-done.1
  177.4 2.0 %fusion = f32[1,336,1344]{2,1,0:T(8,128)} fusion(bf16[336,512]{1,0:T(8,128)(2,1)S(1)} %fusion.7, bf16[1344,512]{1,0:T(8,128)(2,1)S(1)} %copy-done.1), kind=kOutput, calls=%fused_computation.1 | convolution fusion | flops 462873600 | bytes 3526656 | tf_op jit(solution)/shard_map/dot_general | solution.py:44
Async XLA Ops:
  7.2 1.6 copy-start
  7.2 117.3 %all-reduce.2.cloned.1.call-start = ((), (), s32[]{:S(2)}) async-start(), calls=%async_computation.1 | async-start | bytes 5505024 | tf_op jit(solution)/shard_map/psum | solution.py:15
  13.3 111.2 %copy-start.2 = (f32[1,168,1024]{2,1,0:T(8,128)S(1)}, f32[1,168,1024]{2,1,0:T(8,128)}, u32[]{:S(2)}) copy-start(f32[1,168,1024]{2,1,0:T(8,128)} %param.10) | copy-start | bytes 2064388
  13.3 111.2 %copy-start.3 = (bf16[1,168,1024]{2,1,0:T(8,128)(2,1)S(1)}, bf16[1,168,1024]{2,1,0:T(8,128)(2,1)}, u32[]{:S(2)}) copy-start(bf16[1,168,1024]{2,1,0:T(8,128)(2,1)} %param.9) | copy-start | bytes 1032196
  13.3 162.5 %all-gather.3.cloned.1.call-start = ((), (), s32[]{:S(2)}) async-start(), calls=%async_computation.2 | async-start | bytes 1720320 | tf_op jit(solution)/shard_map/all_gather | solution.py:35
  13.4 124.5 %copy-start.4 = (bf16[1,128,512]{2,1,0:T(8,128)(2,1)S(1)}, bf16[1,128,512]{2,1,0:T(8,128)(2,1)}, u32[]{:S(2)}) copy-start(bf16[1,128,512]{2,1,0:T(8,128)(2,1)} %param.11) | copy-start | bytes 393220
  175.8 1.6 copy-start.1
Sparse Core Ops, SparseCore 0:
  13.4 111.0 all-reduce.1
  137.9 37.8 all-gather.2
where the time goes:
time: 187 us; the launch traced here: 186 us
  waiting for transfers between devices  127 us (68%)
  blocking collectives  31.8 us (17%)
  between operations  14.9 us (8%)
  matrix products  8.09 us (4%)
  local copies, waits for them, and re-layouts  3.44 us (2%)
    psum x1, waiting for transfers between devices, shards(): lax.psum(jnp.dot(amp_block, weights, preferred_element_type=jnp.float32)...  111 us
    all_gather x1, blocking collectives, shards(): lax.all_gather(cycle_weights, 'kvir', axis=0, tiled=True)  20.6 us
    all_gather x1, waiting for transfers between devices, shards(): lax.all_gather(local_cycle, 'kvir', axis=1, tiled=True)  15.5 us
    all_to_all x1, blocking collectives, shards(): lax.all_to_all(updated.reshape(rows_dev, tot_count, col_width), 'ktot', s...  11.3 us
    dot_general x1, matrix products, shards(): jnp.dot(amp_block, weights, preferred_element_type=jnp.float32) * scale_mask  4.5 us
  transfers between devices with their start and end apart: 2, of which 2 were waited for; matrix products, arithmetic and copies ran while one was open for 1% of the time, Pallas kernels for 0%

commit v1 on v0

v1 whole, which is shorter than its diff:
```python
import functools
import jax
import jax.numpy as jnp
from jax import lax
from jax.sharding import PartitionSpec as P
from jax.experimental import pallas as pl
from jax.experimental.pallas import tpu as pltpu

MESH = pl.DeviceIdType.MESH


def pieces_of(rows):
    for pieces in (3, 7, 2, 1):
        if rows % (8 * pieces) == 0:
            return pieces
    return 1


def kernel(
    nq, nv, nc,
    amp_ref, int_ref, mark_ref, cur_ref, den_ref, cyc_ref,
    lad_ref, out_ref,
    part, left, right, send_p, send_m, upd, got, mixbuf, cyc, full, weights,
    s_p, r_p, s_m, r_m, s_a, r_a, s_cr, s_cl, r_c, s_wr, s_wl, r_w,
):
    me = lax.axis_index("ktot")
    z = lax.axis_index("kvir")
    rc = cur_ref.shape[1]
    cw = upd.shape[3]
    has_left = z > 0
    has_right = z < nv - 1

    def peer(i):
        return lax.rem(me + i, nq)

    barrier = pltpu.get_barrier_semaphore()

    @pl.when(has_left)
    def _():
        pl.semaphore_signal(barrier, inc=1, device_id=(me, z - 1), device_id_type=MESH)

    @pl.when(has_right)
    def _():
        pl.semaphore_signal(barrier, inc=1, device_id=(me, z + 1), device_id_type=MESH)

    for i in range(1, nq):
        pl.semaphore_signal(barrier, inc=1, device_id=(peer(i), z), device_id_type=MESH)
    pl.semaphore_wait(
        barrier, nq - 1 + has_left.astype(jnp.int32) + has_right.astype(jnp.int32))

    def to(ref, there, send, recv, k, v):
        return pltpu.make_async_remote_copy(
            src_ref=ref, dst_ref=there, send_sem=send, recv_sem=recv,
            device_id=(k, v), device_id_type=MESH)

    def plus(d, j):
        return to(send_p.at[d, j], left.at[d, j], s_p.at[d, j], r_p.at[d, j], me, z + 1)

    def minus(d, j):
        return to(send_m.at[d, j], right.at[d, j], s_m.at[d, j], r_m.at[d, j], me, z - 1)

    def exchange(i, j):
        return to(upd.at[j, peer(i)], got.at[j, me], s_a.at[j, i], r_a.at[j, me], peer(i), z)

    def exchange_in(i, j):
        k = lax.rem(me + nq - i, nq)
        return to(upd.at[j, k], got.at[j, k], s_a.at[j, i], r_a.at[j, k], peer(i), z)

    def spread(v, j, right_way):
        rows = pl.ds(j * rc * nq, rc * nq)
        ref = cyc.at[v, rows]
        return to(ref, ref, (s_cr if right_way else s_cl).at[v, j], r_c.at[v, j], me,
                  z + 1 if right_way else z - 1)

    def wspread(v, right_way):
        ref = weights.at[v]
        return to(ref, ref, (s_wr if right_way else s_wl).at[v], r_w.at[v], me,
                  z + 1 if right_way else z - 1)

    def send_both(make):
        @pl.when(has_right)
        def _():
            make(True).start()

        @pl.when(has_left)
        def _():
            make(False).start()

    weights[z] = cyc_ref[...]
    send_both(lambda way: wspread(z, way))

    mark = mark_ref[0, 0].astype(jnp.float32)

    def ladder_block(i, carry):
        d = jnp.where(z < nv // 2, nv - 1 - i, i)
        part[d] = jnp.dot(amp_ref[d], int_ref[...], preferred_element_type=jnp.float32) * mark
        return carry

    lax.fori_loop(0, nv, ladder_block, 0)

    def mine(d, j):
        return part[d, j * rc:(j + 1) * rc, :]

    def reduce_plus(d, j):
        @pl.when(z == 0)
        def _():
            send_p[d, j] = mine(d, j).astype(jnp.bfloat16)

        @pl.when(has_left & (z < d))
        def _():
            plus(d, j).wait_recv()
            send_p[d, j] = (mine(d, j) + left[d, j].astype(jnp.float32)).astype(jnp.bfloat16)

        @pl.when(z < d)
        def _():
            plus(d, j).start()

    def reduce_minus(d, j):
        @pl.when(z == nv - 1)
        def _():
            send_m[d, j] = mine(d, j).astype(jnp.bfloat16)

        @pl.when(has_right & (z > d))
        def _():
            minus(d, j).wait_recv()
            send_m[d, j] = (mine(d, j) + right[d, j].astype(jnp.float32)).astype(jnp.bfloat16)

        @pl.when(z > d)
        def _():
            minus(d, j).start()

    def reduce(j):
        for i in range(nv - 1):
            reduce_plus(nv - 1 - i, j)
            reduce_minus(i, j)

    def finish(j):
        @pl.when(has_left)
        def _():
            plus(z, j).wait_recv()
            part[z, j * rc:(j + 1) * rc, :] += left[z, j].astype(jnp.float32)

        @pl.when(has_right)
        def _():
            minus(z, j).wait_recv()
            part[z, j * rc:(j + 1) * rc, :] += right[z, j].astype(jnp.float32)

        total = mine(z, j)
        lad_ref[j] = total.astype(jnp.bfloat16)
        new = (cur_ref[j].astype(jnp.float32) + total / den_ref[j]).astype(jnp.bfloat16)
        for q in range(nq):
            upd[j, q] = new[:, q * cw:(q + 1) * cw]
        for i in range(1, nq):
            exchange(i, j).start()
        got[j, me] = upd[j, me]

    def collect(j):
        for i in range(1, nq):
            exchange_in(i, j).wait_recv()
        for k in range(nq):
            mixbuf[pl.ds(k, rc, stride=nq), :] = got[j, k].astype(jnp.float32)
        cyc[z, j * rc * nq:(j + 1) * rc * nq, :] = mixbuf[...].astype(jnp.bfloat16)
        send_both(lambda way: spread(z, j, way))

    def pass_on(make):
        for h in range(1, nv):
            @pl.when(z - h >= 0)
            def _():
                make(z - h, True).wait_recv()

                @pl.when(has_right)
                def _():
                    make(z - h, True).start()

            @pl.when(z + h < nv)
            def _():
                make(z + h, False).wait_recv()

                @pl.when(has_left)
                def _():
                    make(z + h, False).start()

    for s in range(nc + 2):
        if s < nc:
            reduce(s)
        if s == 0:
            pass_on(wspread)
        if 0 <= s - 1 < nc:
            collect(s - 1)
        if s < nc:
            finish(s)
        if 0 <= s - 2 < nc:
            pass_on(lambda v, way: spread(v, s - 2, way))

    for v in range(nv):
        full[:, v * cw:(v + 1) * cw] = cyc[v]
    share = full.shape[0] // nv
    start = pl.multiple_of(z * share, share)
    mixed = jnp.zeros((share, cyc_ref.shape[1]), jnp.float32)
    for v in range(nv):
        term = jnp.dot(cyc[v, pl.ds(start, share), :], weights[v], preferred_element_type=jnp.float32)
        mixed = mixed + term.astype(jnp.bfloat16).astype(jnp.float32)
    result = lax.dot_general(
        mixed.astype(jnp.bfloat16), full[...], (((1,), (1,)), ((), ())),
        preferred_element_type=jnp.float32)
    out_ref[...] = result * cyc_ref.shape[1] ** (-0.5)

    for j in range(nc):
        for d in range(nv):
            @pl.when(z < d)
            def _():
                plus(d, j).wait_send()

            @pl.when(z > d)
            def _():
                minus(d, j).wait_send()
        for i in range(1, nq):
            exchange(i, j).wait_send()

    def drain(v, make):
        @pl.when((v <= z) & has_right)
        def _():
            make(v, True).wait_send()

        @pl.when((v >= z) & has_left)
        def _():
            make(v, False).wait_send()

    for v in range(nv):
        drain(v, wspread)
        for j in range(nc):
            drain(v, lambda v, way: spread(v, j, way))


def fused(nq, nv, amplitudes, ladder_integrals, listed, current, denominators, cycle_integrals):
    rows, width = current.shape[1:]
    cw = width // nq
    nc = pieces_of(rows)
    rc = rows // nc
    cycle = cycle_integrals.shape[2]
    yr = rows * nq
    b16, f32 = jnp.bfloat16, jnp.float32
    vmem = pl.BlockSpec(memory_space=pltpu.VMEM)
    dma = pltpu.SemaphoreType.DMA
    lad, out = pl.pallas_call(
        functools.partial(kernel, nq, nv, nc),
        out_shape=(jax.ShapeDtypeStruct((nc, rc, width), b16),
                   jax.ShapeDtypeStruct((yr // nv, yr), f32)),
        in_specs=[vmem, vmem, pl.BlockSpec(memory_space=pltpu.SMEM), vmem, vmem, vmem],
        out_specs=(vmem, vmem),
        scratch_shapes=[
            pltpu.VMEM((nv, rows, width), f32),
            pltpu.VMEM((nv, nc, rc, width), b16),
            pltpu.VMEM((nv, nc, rc, width), b16),
            pltpu.VMEM((nv, nc, rc, width), b16),
            pltpu.VMEM((nv, nc, rc, width), b16),
            pltpu.VMEM((nc, nq, rc, cw), b16),
            pltpu.VMEM((nc, nq, rc, cw), b16),
            pltpu.VMEM((rc * nq, cw), f32),
            pltpu.VMEM((nv, yr, cw), b16),
            pltpu.VMEM((yr, cw * nv), b16),
            pltpu.VMEM((nv, cycle // nv, cycle), b16),
            dma((nv, nc)), dma((nv, nc)), dma((nv, nc)), dma((nv, nc)),
            dma((nc, nq)), dma((nc, nq)),
            dma((nv, nc)), dma((nv, nc)), dma((nv, nc)),
            dma((nv,)), dma((nv,)), dma((nv,)),
        ],
        compiler_params=pltpu.CompilerParams(
            collective_id=0, has_side_effects=True, vmem_limit_bytes=56 * 2 ** 20),
    )(
        amplitudes.reshape(nv, rows, amplitudes.shape[3]),
        ladder_integrals[0, 0],
        listed,
        current.reshape(nc, rc, width),
        denominators.reshape(nc, rc, width),
        cycle_integrals[0],
    )
    return lad.reshape(1, rows, width), out[None]


def general(amplitudes, ladder_integrals, listed, current, denominators, cycle_integrals):
    mark = listed[0, 0].astype(jnp.float32)
    rows, width = current.shape[1:]
    nq = lax.axis_size("ktot")
    nv = lax.axis_size("kvir")
    partial = jnp.dot(amplitudes[0, 0], ladder_integrals[0, 0], preferred_element_type=jnp.float32)
    ladder = lax.psum_scatter(partial * mark, "kvir", scatter_dimension=0, tiled=True)
    updated = (current[0].astype(jnp.float32) + ladder / denominators[0]).astype(jnp.bfloat16)
    cw = width // nq
    received = lax.all_to_all(
        updated.reshape(rows, nq, cw), "ktot", split_axis=1, concat_axis=1, tiled=True)
    local = received.reshape(rows * nq, cw)
    weights = cycle_integrals[0]
    cycle = weights.shape[1]
    share = local.shape[0] // nv
    full = lax.all_gather(local, "kvir", axis=1, tiled=True)
    full_weights = lax.all_gather(weights, "kvir", axis=0, tiled=True)
    mine = lax.dynamic_slice_in_dim(full, lax.axis_index("kvir") * share, share, 0)
    terms = jnp.einsum(
        "svw,vwc->vsc", mine.reshape(share, nv, cw), full_weights.reshape(nv, cw, cycle),
        preferred_element_type=jnp.float32)
    terms = terms.astype(jnp.bfloat16).astype(jnp.float32)
    mixed = jnp.sum(terms, axis=0).astype(jnp.bfloat16)
    out = lax.dot_general(
        mixed, full, (((1,), (1,)), ((), ())), preferred_element_type=jnp.float32)
    return ladder.astype(jnp.bfloat16)[None], (out * cycle ** (-0.5))[None]


def solution(mesh):
    nq, nv = mesh.shape["ktot"], mesh.shape["kvir"]

    def shards(*arrays):
        rows, width = arrays[3].shape[1:]
        share = rows * nq // nv
        fits = (rows % 8 == 0 and width % (128 * nq) == 0 and share % 16 == 0
                and arrays[5].shape[2] == width // nq * nv
                and rows * nv == arrays[0].shape[2])
        return fused(nq, nv, *arrays) if fits else general(*arrays)

    return jax.shard_map(
        shards,
        mesh=mesh,
        in_specs=(
            P("ktot", "kvir", None, None),
            P("ktot", "kvir", None, None),
            P("ktot", "kvir"),
            P("ktot", "kvir", None),
            P("ktot", "kvir", None),
            P("ktot", "kvir", None),
        ),
        out_specs=(P("ktot", "kvir", None), P("ktot", "kvir", None)),
        check_vma=False,
    )
```

time: 187 us -> 93.3 us (0.50)
  waiting for transfers between devices: 127 us -> 0 us
  Pallas kernels: 0 us -> 87.2 us
  blocking collectives: 31.8 us -> 0 us
  between operations: 14.9 us -> 1.28 us
  matrix products: 8.09 us -> 0 us
    psum x1 -> x0, waiting for transfers between devices: 111 us -> none  [shards(): lax.psum(jnp.dot(amp_block, weights, preferred_element_type=jnp.float32)...]
    pallas_call x0 -> x1, Pallas kernels: none -> 87.2 us  [fused(): pl.pallas_call(functools.partial(kernel, nq, nv, nc), out_shape=(jax.Shap...]
    all_gather x1 -> x0, blocking collectives: 20.6 us -> none  [shards(): lax.all_gather(cycle_weights, 'kvir', axis=0, tiled=True)]
    all_gather x1 -> x0, waiting for transfers between devices: 15.5 us -> none  [shards(): lax.all_gather(local_cycle, 'kvir', axis=1, tiled=True)]
    all_to_all x1 -> x0, blocking collectives: 11.3 us -> none  [shards(): lax.all_to_all(updated.reshape(rows_dev, tot_count, col_width), 'ktot', s...]
    dot_general x3 -> x0, matrix products: 8.09 us -> none  [the longest x1 4.5 us: shards(): jnp.dot(amp_block, weights, preferred_element_type=jnp.float32) * scale_mask]
    unnamed x10 -> x2, local copies, waits for them, and re-layouts: 0.79 us -> 4.62 us
    broadcast_in_dim x1 -> x0, local copies, waits for them, and re-layouts: 1.88 us -> none  [shards(): ladder.astype(jnp.bfloat16)[None]]
  transfers between devices with their start and end apart: 2 -> 0, of which waited for: 2 -> 0; matrix products, arithmetic and copies ran while one was open for 1% -> 0% of each run, Pallas kernels for 0% -> 0%
where the time goes in v1:
time: 93.3 us; the launch traced here: 93.1 us
  Pallas kernels  87.2 us (93%)
  local copies, waits for them, and re-layouts  4.62 us (5%)
  between operations  1.28 us (1%)
    pallas_call x1, Pallas kernels, fused(): pl.pallas_call(functools.partial(kernel, nq, nv, nc), out_shape=(jax.Shap...  87.2 us
    unnamed x2, local copies, waits for them, and re-layouts  4.62 us

profile of v1, /device:TPU:0, one launch (start us, length us, event | category | flops | bytes accessed | tf_op | source)
XLA Modules:
  0.0 93.1 jit_solution(2957856091399646991)
XLA Ops:
  1.3 87.2 %shard_map.77 = (bf16[3,56,1024]{2,1,0:T(8,128)(2,1)}, f32[336,1344]{1,0:T(8,128)}) custom-call(bf16[4,168,1024]{2,1,0:T(8,128)(2,1)} %bitcast.9, bf16[1024,1024]{1,0:T(8,128)(2,1)} %bitcast.7, s32[1,1]{1,0:T(1,128)S(6)} %copy.10.mark_ref, bf16[3,56,1024]{2,1,0:T(8,128)(2,1)} %bitcast.12, f32[3,56,1024]{2,1,0:T(8,128)} %bitcast.10, bf16[128,512]{1,0:T(8,128)(2,1)} %bitcast.13), custom_call_target="tpu_custom_call" | custom-call | tf_op jit(solution)/shard_map/pallas_call | solution.py:245
  88.5 1.7 %copy.11 = bf16[1,168,1024]{2,1,0:T(8,128)(2,1)} copy(bf16[1,168,1024]{2,1,0:T(8,128)(2,1)} %bitcast.11) | data formatting | bytes 688128
  90.3 2.9 %copy.12 = f32[1,336,1344]{2,1,0:T(8,128)} copy(f32[1,336,1344]{2,1,0:T(8,128)} %bitcast.8) | data formatting | bytes 3612672

commit v2 on v1

--- a/solution.py
+++ b/solution.py
@@ -6,6 +6,7 @@
 from jax.experimental import pallas as pl
 from jax.experimental.pallas import tpu as pltpu
 
+LAGS = (1, 1, 2, 3)
 MESH = pl.DeviceIdType.MESH
 
 
@@ -29,6 +30,8 @@
     cw = upd.shape[3]
     has_left = z > 0
     has_right = z < nv - 1
+    inner = has_left & has_right
+    low = z < nv // 2
 
     def peer(i):
         return lax.rem(me + i, nq)
@@ -91,48 +94,51 @@
 
     mark = mark_ref[0, 0].astype(jnp.float32)
 
-    def ladder_block(i, carry):
-        d = jnp.where(z < nv // 2, nv - 1 - i, i)
-        part[d] = jnp.dot(amp_ref[d], int_ref[...], preferred_element_type=jnp.float32) * mark
-        return carry
-
-    lax.fori_loop(0, nv, ladder_block, 0)
-
     def mine(d, j):
         return part[d, j * rc:(j + 1) * rc, :]
 
+    def end_send(d, j):
+        @pl.when((z == 0) & (d > 0))
+        def _():
+            send_p[d, j] = mine(d, j).astype(jnp.bfloat16)
+            plus(d, j).start()
+
+        @pl.when((z == nv - 1) & (d < nv - 1))
+        def _():
+            send_m[d, j] = mine(d, j).astype(jnp.bfloat16)
+            minus(d, j).start()
+
+    def ladder_block(i, carry):
+        d = jnp.where(low, nv - 1 - i, i)
+        part[d] = jnp.dot(amp_ref[d], int_ref[...], preferred_element_type=jnp.float32) * mark
+        end_send(d, 0)
+        return carry
+
+    lax.fori_loop(0, nv, ladder_block, 0)
+
     def reduce_plus(d, j):
-        @pl.when(z == 0)
-        def _():
-            send_p[d, j] = mine(d, j).astype(jnp.bfloat16)
-
-        @pl.when(has_left & (z < d))
-        def _():
-            plus(d, j).wait_recv()
-            send_p[d, j] = (mine(d, j) + left[d, j].astype(jnp.float32)).astype(jnp.bfloat16)
-
-        @pl.when(z < d)
-        def _():
-            plus(d, j).start()
+        plus(d, j).wait_recv()
+        send_p[d, j] = (mine(d, j) + left[d, j].astype(jnp.float32)).astype(jnp.bfloat16)
+        plus(d, j).start()
 
     def reduce_minus(d, j):
-        @pl.when(z == nv - 1)
-        def _():
-            send_m[d, j] = mine(d, j).astype(jnp.bfloat16)
-
-        @pl.when(has_right & (z > d))
-        def _():
-            minus(d, j).wait_recv()
-            send_m[d, j] = (mine(d, j) + right[d, j].astype(jnp.float32)).astype(jnp.bfloat16)
-
-        @pl.when(z > d)
-        def _():
-            minus(d, j).start()
-
-    def reduce(j):
+        minus(d, j).wait_recv()
+        send_m[d, j] = (mine(d, j) + right[d, j].astype(jnp.float32)).astype(jnp.bfloat16)
+        minus(d, j).start()
+
+    def reduce(j, near):
+        up = inner & (low if near else jnp.logical_not(low))
+        down = inner & (jnp.logical_not(low) if near else low)
         for i in range(nv - 1):
-            reduce_plus(nv - 1 - i, j)
-            reduce_minus(i, j)
+            p, m = nv - 1 - i, i
+
+            @pl.when(up & (z < p))
+            def _():
+                reduce_plus(p, j)
+
+            @pl.when(down & (z > m))
+            def _():
+                reduce_minus(m, j)
 
     def finish(j):
         @pl.when(has_left)
@@ -162,9 +168,9 @@
         cyc[z, j * rc * nq:(j + 1) * rc * nq, :] = mixbuf[...].astype(jnp.bfloat16)
         send_both(lambda way: spread(z, j, way))
 
-    def pass_on(make):
+    def pass_on(make, wanted):
         for h in range(1, nv):
-            @pl.when(z - h >= 0)
+            @pl.when(wanted(z - h) & (z - h >= 0))
             def _():
                 make(z - h, True).wait_recv()
 
@@ -172,7 +178,7 @@
                 def _():
                     make(z - h, True).start()
 
-            @pl.when(z + h < nv)
+            @pl.when(wanted(z + h) & (z + h < nv))
             def _():
                 make(z + h, False).wait_recv()
 
@@ -180,17 +186,43 @@
                 def _():
                     make(z + h, False).start()
 
-    for s in range(nc + 2):
+    def from_inner(v):
+        return inner & (v > 0) & (v < nv - 1)
+
+    def from_end(near):
+        def wanted(v):
+            return inner & jnp.where(low == near, v == 0, v == nv - 1)
+        return wanted
+
+    def at_end(v):
+        return jnp.logical_not(inner) & (v == v)
+
+    for j in range(1, nc):
+        for i in range(1, nv):
+            end_send(jnp.where(low, nv - i, i - 1), j)
+
+    far, closing, gathering, passing = LAGS
+    for s in range(nc + passing):
         if s < nc:
-            reduce(s)
+            reduce(s, True)
         if s == 0:
-            pass_on(wspread)
-        if 0 <= s - 1 < nc:
-            collect(s - 1)
+            pass_on(wspread, lambda v: inner & (v == v))
+        if 0 <= s - gathering < nc:
+            collect(s - gathering)
+        if 0 <= s - far < nc:
+            reduce(s - far, False)
+        if 0 <= s - closing < nc:
+            finish(s - closing)
+        if 0 <= s - passing < nc:
+            pass_on(lambda v, way: spread(v, s - passing, way), from_inner)
+    for s in range(nc + far):
         if s < nc:
-            finish(s)
-        if 0 <= s - 2 < nc:
-            pass_on(lambda v, way: spread(v, s - 2, way))
+            pass_on(lambda v, way: spread(v, s, way), from_end(True))
+        if 0 <= s - far < nc:
+            pass_on(lambda v, way: spread(v, s - far, way), from_end(False))
+    pass_on(wspread, at_end)
+    for j in range(nc):
+        pass_on(lambda v, way: spread(v, j, way), at_end)
 
     for v in range(nv):
         full[:, v * cw:(v + 1) * cw] = cyc[v]

time: 93.3 us -> 69.5 us (0.74)
  Pallas kernels: 87.2 us -> 63.4 us
    pallas_call x1, Pallas kernels: 87.2 us -> 63.4 us  [fused(): pl.pallas_call(functools.partial(kernel, nq, nv, nc), out_shape=(jax.Shap...]
where the time goes in v2:
time: 69.5 us; the launch traced here: 69.3 us
  Pallas kernels  63.4 us (91%)
  local copies, waits for them, and re-layouts  4.62 us (7%)
  between operations  1.28 us (2%)
    pallas_call x1, Pallas kernels, fused(): pl.pallas_call(functools.partial(kernel, nq, nv, nc), out_shape=(jax.Shap...  63.4 us
    unnamed x2, local copies, waits for them, and re-layouts  4.62 us

profile of v2, /device:TPU:0, one launch (start us, length us, event | category | flops | bytes accessed | tf_op | source)
XLA Modules:
  0.0 69.3 jit_solution(16092351474012169583)
XLA Ops:
  1.3 63.4 %shard_map.77 = (bf16[3,56,1024]{2,1,0:T(8,128)(2,1)}, f32[336,1344]{1,0:T(8,128)}) custom-call(bf16[4,168,1024]{2,1,0:T(8,128)(2,1)} %bitcast.9, bf16[1024,1024]{1,0:T(8,128)(2,1)} %bitcast.7, s32[1,1]{1,0:T(1,128)S(6)} %copy.10.mark_ref, bf16[3,56,1024]{2,1,0:T(8,128)(2,1)} %bitcast.12, f32[3,56,1024]{2,1,0:T(8,128)} %bitcast.10, bf16[128,512]{1,0:T(8,128)(2,1)} %bitcast.13), custom_call_target="tpu_custom_call" | custom-call | tf_op jit(solution)/shard_map/pallas_call | solution.py:277
  64.7 1.7 %copy.11 = bf16[1,168,1024]{2,1,0:T(8,128)(2,1)} copy(bf16[1,168,1024]{2,1,0:T(8,128)(2,1)} %bitcast.11) | data formatting | bytes 688128
  66.4 2.9 %copy.12 = f32[1,336,1344]{2,1,0:T(8,128)} copy(f32[1,336,1344]{2,1,0:T(8,128)} %bitcast.8) | data formatting | bytes 3612672
